TPU v7x, 32 devices: a whole 2x2x4 slice. The times are simulated.
32 devices in a mesh: groups: 2 (over x), depth: 16 (over z, y, core).
Axes of the slice: x: 2, y: 2, z: 4, core: 2. Of those that a mesh axis runs over, the one named last changes fastest.
Arguments:
- alignment_token_grid: int32 [64, 256], P(('groups', 'depth')), parts along dimension 0, may hold values from 0 to 32
- residue_chain_index: int32 [512], P('groups'), parts along dimension 0, may hold values from 0 to 1, as said below
- alignment_state: bfloat16 [64, 256, 768], P(('groups', 'depth')), parts along dimension 0, may hold values from -6 to 6
- embedding: bfloat16 [33, 768], replicated, may hold values from -6 to 6
- chain_head_bias: float32 [2, 12], replicated, may hold values from -2 to 2
- row_query_key_value: bfloat16 [768, 2304], replicated
- row_output_weight: bfloat16 [768, 768], replicated, may hold values from -0.21875 to 0.21875
- column_query_key_value: bfloat16 [768, 2304], replicated
- column_output_weight: bfloat16 [768, 768], replicated, may hold values from -0.21875 to 0.21875
- feed_up_weight: bfloat16 [768, 3072], P('depth'), may hold values from -0.21875 to 0.21875
- feed_down_weight: bfloat16 [3072, 768], P('depth'), may hold values from -0.109375 to 0.109375
Outputs:
- layer_out: bfloat16 [64, 256, 768], P('groups', 'depth'), parts along dimension 0
There are 2 independent parts, one for each index of `groups`. A program takes and returns all parts, laid end to end along the dimension named above; an argument that names none is the same for every part. Nothing has to cross between parts.
Inputs may be any that keep to these rules, and one draw needn't show every extreme that they name: `residue_chain_index`: the residues of the first chain come first, then those of the second; each chain holds 64 to 192 residues.
All inputs are finite; a program needn't handle non-finite values.
Results may differ from a plain program's by a relative error of at most 0.007.
Values may be sent and summed in bfloat16 or wider, within the bound.
A program may use at most 128 MiB of HBM per device.

v0:
```python
import functools
import math

import jax
import jax.numpy as jnp
from jax import lax
from jax.experimental import pallas as pl
from jax.experimental.pallas import tpu as pltpu
from jax.sharding import PartitionSpec as P

MESH = pl.DeviceIdType.MESH
BF = jnp.bfloat16
F32 = jnp.float32


def dot(a, b):
    return jnp.dot(a, b, preferred_element_type=F32)


def dot_t(a, b):
    return lax.dot_general(a, b, (((1,), (1,)), ((), ())), preferred_element_type=F32)


def half_masks(width):
    lane = lax.broadcasted_iota(jnp.int32, (1, width), 1)
    low = jnp.where(lane < width // 2, 1.0, 0.0)
    return low.astype(BF), (1.0 - low).astype(BF)


def project_into(source, weight_ref, target_ref, step):
    def body(t, carry):
        cols = pl.ds(pl.multiple_of(t * step, step), step)
        target_ref[:, cols] = dot(source, weight_ref[:, cols]).astype(BF)
        return carry

    lax.fori_loop(0, weight_ref.shape[1] // step, body, 0)


def row_kernel(
    n, seqs, length, heads, head_size,
    tok_ref, chain_col, chain_row, state_ref, emb_ref, bias_ref, wqkv_ref, wo_ref,
    out_ref,
    x0_ref, qkv_ref, sbuf, rbuf, tbuf, gbuf, pbuf, mix_ref, xbuf,
    pair_sems, rs_send, rs_recv, ag_send, ag_recv, fw_send, fw_recv, aa_send, aa_recv, local_sem,
):
    me = lax.axis_index("depth")
    core = lax.rem(me, 2)
    chip = me // 2
    chips = n // 2
    sibling = me + 1 - 2 * core
    share = length // n
    width = heads * head_size

    barrier = pltpu.get_barrier_semaphore()

    def greet(k, carry):
        pl.semaphore_signal(
            barrier, inc=1, device_id={"depth": lax.rem(me + k, n)}, device_id_type=MESH
        )
        return carry

    lax.fori_loop(1, n, greet, 0)

    letters = lax.broadcasted_iota(jnp.int32, (seqs * length, emb_ref.shape[0]), 1)
    one_hot = jnp.where(tok_ref[...] == letters, 1.0, 0.0).astype(BF)
    x0_ref[...] = state_ref[...].astype(F32) + dot(one_hot, emb_ref[...])
    u1 = layer_norm(x0_ref[...]).astype(BF)
    project_into(u1, wqkv_ref, qkv_ref, 256)
    low, high = half_masks(2 * head_size)

    def pair_cols(which, p):
        cols = pl.ds(pl.multiple_of(which * width + p * 2 * head_size, 2 * head_size), 2 * head_size)
        return [qkv_ref[pl.ds(s * length, length), cols] for s in range(seqs)]

    def scores(p, carry):
        q = pair_cols(0, p)
        k = jnp.concatenate(pair_cols(1, p), axis=1)
        for half, mask in ((0, low), (1, high)):
            part = dot_t(jnp.concatenate([x * mask for x in q], axis=1), k)
            part = part.astype(BF).reshape(chips, 2, share, length)
            for c in range(2):
                sbuf[c, :, 2 * p + half] = part[:, c]
        return carry

    lax.fori_loop(0, heads // 2, scores, 0)
    pl.semaphore_wait(barrier, n - 1)

    swap = pltpu.make_async_remote_copy(
        src_ref=sbuf.at[1 - core], dst_ref=rbuf, send_sem=pair_sems.at[0], recv_sem=pair_sems.at[1],
        device_id={"depth": sibling}, device_id_type=MESH,
    )
    swap.start()
    swap.wait()

    def rs_copy(k):
        other = lax.rem(chip + k, chips)
        return pltpu.make_async_remote_copy(
            src_ref=tbuf.at[other], dst_ref=gbuf.at[k], send_sem=rs_send.at[k], recv_sem=rs_recv.at[k],
            device_id={"depth": other * 2 + core}, device_id_type=MESH,
        )

    def rs_start(k, carry):
        other = lax.rem(chip + k, chips)
        tbuf[other] = (sbuf[core, other].astype(F32) + rbuf[other].astype(F32)).astype(BF)
        rs_copy(k).start()
        return carry

    lax.fori_loop(1, chips, rs_start, 0)
    total = sbuf[core, chip].astype(F32) + rbuf[chip].astype(F32)

    def rs_add(k, total):
        rs_copy(k).wait_recv()
        return total + gbuf[k].astype(F32)

    total = lax.fori_loop(1, chips, rs_add, total)
    factor = 1.0 / (math.sqrt(head_size) * math.sqrt(seqs * n))
    mine = chain_col[pl.ds(pl.multiple_of(me * share, share), share), :]
    same = mine == chain_row[...]
    for h in range(heads):
        tied = total[h] * factor + jnp.where(same, bias_ref[1, h], bias_ref[0, h])
        top = jnp.max(tied, axis=-1, keepdims=True)
        weights = jnp.exp(tied - top)
        pbuf[me, h] = (weights / jnp.sum(weights, axis=-1, keepdims=True)).astype(BF)

    def ag_copy(k):
        other = lax.rem(chip + k, chips)
        return pltpu.make_async_remote_copy(
            src_ref=pbuf.at[me], dst_ref=pbuf.at[me], send_sem=ag_send.at[k], recv_sem=ag_recv.at[k],
            device_id={"depth": other * 2 + core}, device_id_type=MESH,
        )

    def fw_copy(k):
        origin = lax.rem(chip - k + chips, chips) * 2 + core
        return pltpu.make_async_remote_copy(
            src_ref=pbuf.at[origin], dst_ref=pbuf.at[origin], send_sem=fw_send.at[k], recv_sem=fw_recv.at[k],
            device_id={"depth": sibling}, device_id_type=MESH,
        )

    def ag_start(k, carry):
        ag_copy(k).start()
        return carry

    lax.fori_loop(1, chips, ag_start, 0)
    fw_copy(0).start()

    def ag_forward(k, carry):
        ag_copy(k).wait_recv()
        fw_copy(k).start()
        return carry

    lax.fori_loop(1, chips, ag_forward, 0)

    def fw_wait(k, carry):
        fw_copy(k).wait_recv()
        return carry

    lax.fori_loop(0, chips, fw_wait, 0)

    def mixing(p, carry):
        v = jnp.concatenate(pair_cols(2, p), axis=1)
        lows = jnp.concatenate([low] * seqs, axis=1)
        highs = jnp.concatenate([high] * seqs, axis=1)
        keys = jnp.concatenate([v * lows, v * highs], axis=0)
        probs = jnp.concatenate(
            [pbuf[:, 2 * p].reshape(length, length), pbuf[:, 2 * p + 1].reshape(length, length)], axis=1
        )
        mixed = dot(probs, keys).astype(BF)
        pair = 2 * head_size
        cols = pl.ds(pl.multiple_of(p * pair, pair), pair)
        for s in range(seqs):
            mix_ref[pl.ds(s * length, length), cols] = mixed[:, s * pair : (s + 1) * pair]
        return carry

    lax.fori_loop(0, heads // 2, mixing, 0)

    def finish(t, carry):
        cols = pl.ds(pl.multiple_of(t * 256, 256), 256)
        x1 = (x0_ref[:, cols] + dot(mix_ref[...], wo_ref[:, cols])).astype(BF)
        for s in range(seqs):
            xbuf[:, s, :, cols] = x1[s * length : (s + 1) * length].reshape(n, share, 256)
        return carry

    lax.fori_loop(0, width // 256, finish, 0)

    def aa_copy(k):
        other = lax.rem(me + k, n)
        return pltpu.make_async_remote_copy(
            src_ref=xbuf.at[other], dst_ref=out_ref.at[me], send_sem=aa_send.at[k], recv_sem=aa_recv.at[k],
            device_id={"depth": other}, device_id_type=MESH,
        )

    def aa_start(k, carry):
        aa_copy(k).start()
        return carry

    lax.fori_loop(1, n, aa_start, 0)
    keep = pltpu.make_async_copy(xbuf.at[me], out_ref.at[me], local_sem)
    keep.start()
    keep.wait()

    def drain(k, carry):
        aa_copy(k).wait()
        return carry

    lax.fori_loop(1, n, drain, 0)

    def drain_sends(k, carry):
        rs_copy(k).wait_send()
        ag_copy(k).wait_send()
        fw_copy(k).wait_send()
        return carry

    lax.fori_loop(1, chips, drain_sends, 0)
    fw_copy(0).wait_send()


def column_order(rows, all_seqs, cols, inverse):
    r = lax.broadcasted_iota(jnp.int32, (rows, rows), 0)
    c = lax.broadcasted_iota(jnp.int32, (rows, rows), 1)
    if inverse:
        r, c = c, r
    return jnp.where(c == (r % all_seqs) * cols + r // all_seqs, 1.0, 0.0).astype(BF)


def column_kernel(
    all_seqs, heads, head_size, x_ref, wqkv_ref, wo_ref, x2_ref, u3_ref, flat_ref, qkv_ref, mix_ref
):
    rows, width = x_ref.shape
    cols = rows // all_seqs
    flat_ref[...] = dot(column_order(rows, all_seqs, cols, False), x_ref[...])
    u2 = layer_norm(flat_ref[...]).astype(BF)
    project_into(u2, wqkv_ref, qkv_ref, 256)
    pair = 2 * head_size
    low, high = half_masks(pair)
    group = 128
    r = lax.broadcasted_iota(jnp.int32, (2 * group, group), 0)
    c = lax.broadcasted_iota(jnp.int32, (2 * group, group), 1)
    inside = (r % group) // all_seqs == c // all_seqs
    factor = 1.0 / math.sqrt(head_size)

    def attend(g, carry):
        here = pl.ds(pl.multiple_of(g * group, group), group)
        for p in range(heads // 2):
            q = qkv_ref[here, p * pair : (p + 1) * pair]
            k = qkv_ref[here, width + p * pair : width + (p + 1) * pair]
            v = qkv_ref[here, 2 * width + p * pair : 2 * width + (p + 1) * pair]
            scores = dot_t(jnp.concatenate([q * low, q * high], axis=0), k) * factor
            scores = jnp.where(inside, scores, -jnp.inf)
            top = jnp.max(scores, axis=-1, keepdims=True)
            weights = jnp.exp(scores - top)
            probs = (weights / jnp.sum(weights, axis=-1, keepdims=True)).astype(BF)
            probs = jnp.concatenate([probs[:group], probs[group:]], axis=1)
            values = jnp.concatenate([v * low, v * high], axis=0)
            mix_ref[here, p * pair : (p + 1) * pair] = dot(probs, values).astype(BF)
        return carry

    lax.fori_loop(0, rows // group, attend, 0)
    x2_ref[...] = flat_ref[...] + dot(mix_ref[...], wo_ref[...])
    u3_ref[...] = layer_norm(x2_ref[...]).astype(BF)


def feed_kernel(all_seqs, x2_ref, u3_ref, up_ref, down_ref, out_ref, acc_ref):
    rows = x2_ref.shape[0]
    acc_ref[...] = x2_ref[...]
    step = 512

    def body(t, carry):
        part = pl.ds(pl.multiple_of(t * step, step), step)
        pre = dot(u3_ref[...], up_ref[:, part])
        hidden = (0.5 * pre * (1.0 + lax.erf(pre * math.sqrt(0.5)))).astype(BF)
        acc_ref[...] += dot(hidden, down_ref[part, :])
        return carry

    lax.fori_loop(0, up_ref.shape[1] // step, body, 0)
    order = column_order(rows, all_seqs, rows // all_seqs, True)
    out_ref[...] = dot(order, acc_ref[...].astype(BF)).astype(BF)


def vmem_specs(count):
    return [pl.BlockSpec(memory_space=pltpu.VMEM)] * count


def fast_device(
    alignment_token_grid,
    residue_chain_index,
    alignment_state,
    embedding,
    chain_head_bias,
    row_query_key_value,
    row_output_weight,
    column_query_key_value,
    column_output_weight,
    feed_up_weight,
    feed_down_weight,
):
    seqs, length, width = alignment_state.shape
    heads = chain_head_bias.shape[1]
    head_size = width // heads
    n = lax.axis_size("depth")
    share = length // n
    rows = seqs * length
    all_seqs = seqs * n
    full_up = lax.all_gather(feed_up_weight, "depth", axis=0, tiled=True)
    full_down = lax.all_gather(feed_down_weight, "depth", axis=0, tiled=True)
    chunk = (heads, share, length)
    DMA = pltpu.SemaphoreType.DMA
    block = pl.pallas_call(
        functools.partial(row_kernel, n, seqs, length, heads, head_size),
        out_shape=jax.ShapeDtypeStruct((n, seqs, share, width), BF),
        in_specs=vmem_specs(5) + [pl.BlockSpec(memory_space=pltpu.SMEM)] + vmem_specs(2),
        out_specs=pl.BlockSpec(memory_space=pltpu.VMEM),
        scratch_shapes=[
            pltpu.VMEM((rows, width), F32),
            pltpu.VMEM((rows, 3 * width), BF),
            pltpu.VMEM((2, n // 2) + chunk, BF),
            pltpu.VMEM((n // 2,) + chunk, BF),
            pltpu.VMEM((n // 2,) + chunk, BF),
            pltpu.VMEM((n // 2,) + chunk, BF),
            pltpu.VMEM((n,) + chunk, BF),
            pltpu.VMEM((rows, width), BF),
            pltpu.VMEM((n, seqs, share, width), BF),
            DMA((2,)),
            DMA((n // 2,)), DMA((n // 2,)), DMA((n // 2,)), DMA((n // 2,)),
            DMA((n // 2,)), DMA((n // 2,)), DMA((n,)), DMA((n,)), DMA,
        ],
        compiler_params=pltpu.CompilerParams(
            collective_id=0, has_side_effects=True, vmem_limit_bytes=40 * 2**20
        ),
        cost_estimate=pl.CostEstimate(
            flops=2 * rows * width * width * 5, bytes_accessed=200 * 2**20, transcendentals=0
        ),
        name="row_stage",
    )(
        alignment_token_grid.reshape(rows, 1),
        residue_chain_index.reshape(length, 1),
        residue_chain_index.reshape(1, length),
        alignment_state.reshape(rows, width),
        embedding,
        chain_head_bias,
        row_query_key_value,
        row_output_weight,
    )
    x2, u3 = pl.pallas_call(
        functools.partial(column_kernel, all_seqs, heads, head_size),
        out_shape=(jax.ShapeDtypeStruct((rows, width), F32), jax.ShapeDtypeStruct((rows, width), BF)),
        in_specs=vmem_specs(3),
        out_specs=(pl.BlockSpec(memory_space=pltpu.VMEM),) * 2,
        scratch_shapes=[
            pltpu.VMEM((rows, width), F32),
            pltpu.VMEM((rows, 3 * width), BF),
            pltpu.VMEM((rows, width), BF),
        ],
        compiler_params=pltpu.CompilerParams(vmem_limit_bytes=40 * 2**20),
        cost_estimate=pl.CostEstimate(
            flops=2 * rows * width * width * 5, bytes_accessed=60 * 2**20, transcendentals=0
        ),
        name="column_stage",
    )(block.reshape(rows, width), column_query_key_value, column_output_weight)
    result = pl.pallas_call(
        functools.partial(feed_kernel, all_seqs),
        out_shape=jax.ShapeDtypeStruct((rows, width), BF),
        in_specs=vmem_specs(4),
        out_specs=pl.BlockSpec(memory_space=pltpu.VMEM),
        scratch_shapes=[pltpu.VMEM((rows, width), F32)],
        compiler_params=pltpu.CompilerParams(vmem_limit_bytes=48 * 2**20),
        cost_estimate=pl.CostEstimate(
            flops=2 * rows * width * width * 8, bytes_accessed=40 * 2**20, transcendentals=0
        ),
        name="feed_stage",
    )(x2, u3, full_up, full_down)
    return result.reshape(all_seqs, share, width)


def layer_norm(values):
    center = values - jnp.mean(values, axis=-1, keepdims=True)
    spread = jnp.mean(center * center, axis=-1, keepdims=True)
    return center * lax.rsqrt(spread + 1e-05)


def chain_terms(query_ids, residue_chain_index, chain_head_bias):
    same = query_ids[:, None] == residue_chain_index[None, :]
    return jnp.where(
        same[:, None, :], chain_head_bias[1][None, :, None], chain_head_bias[0][None, :, None]
    )


def plain_device(
    alignment_token_grid,
    residue_chain_index,
    alignment_state,
    embedding,
    chain_head_bias,
    row_query_key_value,
    row_output_weight,
    column_query_key_value,
    column_output_weight,
    feed_up_weight,
    feed_down_weight,
):
    device_sequences = alignment_state.shape[0]
    residue_length = alignment_state.shape[1]
    hidden_width = alignment_state.shape[2]
    heads = chain_head_bias.shape[1]
    head_size = hidden_width // heads
    devices = lax.axis_size("depth")
    all_seqs = device_sequences * devices
    token_letters = embedding.shape[0]
    one_hot = (
        alignment_token_grid.reshape(-1)[:, None]
        == jnp.arange(token_letters, dtype=jnp.int32)[None, :]
    ).astype(jnp.bfloat16)
    initial_input0 = alignment_state.reshape(-1, hidden_width).astype(jnp.float32) + jnp.dot(
        one_hot, embedding, preferred_element_type=jnp.float32
    )
    u1 = layer_norm(initial_input0).astype(jnp.bfloat16)
    qkv1 = jnp.dot(u1, row_query_key_value, preferred_element_type=jnp.float32).astype(jnp.bfloat16)
    qkv1 = qkv1.reshape(device_sequences, residue_length, 3, heads, head_size)
    queries = qkv1[:, :, 0]
    keys_row = qkv1[:, :, 1]
    values_row = qkv1[:, :, 2]
    factor = 1.0 / (math.sqrt(head_size) * math.sqrt(all_seqs))
    partial_value = jnp.einsum(
        "sihd,sjhd->ihj", queries, keys_row, preferred_element_type=jnp.float32
    )
    tied = lax.psum(partial_value, "depth") * factor
    tied = tied + chain_terms(residue_chain_index, residue_chain_index, chain_head_bias)
    row_probs = jax.nn.softmax(tied, axis=-1).astype(jnp.bfloat16)
    row_mix = jnp.einsum(
        "ihj,sjhd->sihd", row_probs, values_row, preferred_element_type=jnp.float32
    ).astype(jnp.bfloat16)
    x1 = initial_input0 + jnp.dot(
        row_mix.reshape(-1, hidden_width), row_output_weight, preferred_element_type=jnp.float32
    )
    col_share = residue_length // devices
    x1 = x1.astype(jnp.bfloat16).reshape(device_sequences, devices, col_share, hidden_width)
    block = lax.all_to_all(x1, "depth", split_axis=1, concat_axis=0, tiled=True)
    seqs_here = block.shape[0]
    cols = block.shape[2]
    flat = block.reshape(seqs_here * cols, hidden_width).astype(jnp.float32)
    u2 = layer_norm(flat).astype(jnp.bfloat16)
    qkv2 = jnp.dot(u2, column_query_key_value, preferred_element_type=jnp.float32).astype(
        jnp.bfloat16
    )
    qkv2 = qkv2.reshape(seqs_here, cols, 3, heads, head_size)
    scores = jnp.einsum(
        "snhd,tnhd->nhst", qkv2[:, :, 0], qkv2[:, :, 1], preferred_element_type=jnp.float32
    ) / math.sqrt(head_size)
    col_probs = jax.nn.softmax(scores, axis=-1).astype(jnp.bfloat16)
    col_mix = jnp.einsum(
        "nhst,tnhd->snhd", col_probs, qkv2[:, :, 2], preferred_element_type=jnp.float32
    ).astype(jnp.bfloat16)
    result = flat + jnp.dot(
        col_mix.reshape(seqs_here * cols, hidden_width),
        column_output_weight,
        preferred_element_type=jnp.float32,
    )
    x2 = result.reshape(seqs_here, 1, cols, hidden_width)
    out_shape = (x2.shape[0], x2.shape[2], hidden_width)
    flat2 = x2.reshape(-1, hidden_width)
    u3 = layer_norm(flat2).astype(jnp.bfloat16)
    full_up, full_down = (
        lax.all_gather(feed_up_weight, "depth", axis=0, tiled=True),
        lax.all_gather(feed_down_weight, "depth", axis=0, tiled=True),
    )
    pre = jnp.dot(u3, full_up, preferred_element_type=jnp.float32)
    hidden = jax.nn.gelu(pre, approximate=False).astype(jnp.bfloat16)
    projected = jnp.dot(hidden, full_down, preferred_element_type=jnp.float32)
    return (flat2 + projected).astype(jnp.bfloat16).reshape(out_shape)


def per_device(*arrays):
    seqs, length, width = arrays[2].shape
    heads = arrays[4].shape[1]
    n = lax.axis_size("depth")
    fits = (
        n % 2 == 0
        and length % n == 0
        and (length // n) % 16 == 0
        and 128 % (seqs * n) == 0
        and (seqs * length) % 128 == 0
        and 2 * (width // heads) == 128
        and heads % 2 == 0
        and width % 256 == 0
    )
    return (fast_device if fits else plain_device)(*arrays)


def solution(mesh):
    in_specs = (
        P(("groups", "depth"), None),
        P("groups"),
        P(("groups", "depth"), None, None),
        P(),
        P(),
        P(),
        P(),
        P(),
        P(),
        P("depth", None),
        P("depth", None),
    )
    out_specs = P("groups", "depth", None)
    return jax.shard_map(
        per_device, mesh=mesh, in_specs=in_specs, out_specs=out_specs, check_vma=False
    )
```

profile of v0, /device:TPU:0, one launch (start us, length us, event | category | flops | bytes accessed | tf_op | source)
XLA Modules:
  0.0 173.8 jit_solution(18314078178502457688)
XLA Ops:
  6.5 0.0 all-gather.3.cloned.1.call-start
  6.5 0.7 all-gather.3.cloned.1.call-update
  7.3 0.0 all-gather.5.cloned.1.call-start
  7.3 0.7 all-gather.5.cloned.1.call-update
  8.0 0.7 copy.14
  8.7 0.1 copy.15
  8.8 0.8 copy.13.chain_col
  9.7 0.0 copy-start
  9.7 0.7 copy-done
  10.3 0.0 copy-start.1
  10.4 2.0 %copy-done.1 = bf16[768,2304]{1,0:T(8,128)(2,1)S(1)} copy-done((bf16[768,2304]{1,0:T(8,128)(2,1)S(1)}, bf16[768,2304]{1,0:T(8,128)(2,1)}, u32[]{:S(2)}) %copy-start.1) | copy-done | bytes 3538968
  12.4 0.0 copy-start.3
  12.4 1.3 copy-done.3
  13.6 0.0 copy-start.5
  13.6 1.1 copy-done.5
  14.8 0.0 copy-start.6
  14.8 0.8 copy-done.6
  15.6 0.0 copy-start.7
  15.6 0.7 copy-done.7
  16.3 0.0 copy-start.2
  16.3 0.0 copy-start.4
  16.3 88.5 %row_stage.1 = bf16[16,2,16,768]{3,2,1,0:T(8,128)(2,1)S(1)} custom-call(s32[512,1]{1,0:T(8,128)S(1)} %bitcast.9, s32[256,1]{1,0:T(8,128)S(1)} %copy.13.chain_col, s32[1,256]{1,0:T(1,128)S(1)} %bitcast.11, bf16[512,768]{1,0:T(8,128)(2,1)S(1)} %bitcast.12, bf16[33,768]{1,0:T(8,128)(2,1)S(1)} %copy-done.6, f32[2,12]{1,0:T(2,128)S(1)} %copy-done.7, ...), custom_call_target="tpu_custom_call" | custom-call | flops 3019898880 | bytes 209715200 | tf_op jit(solution)/shard_map/row_stage/pallas_call | solution.py:307
  104.7 0.0 copy-done.2
  104.7 0.0 copy-done.4
  104.8 9.6 %column_stage.1 = (f32[512,768]{1,0:T(8,128)S(1)}, bf16[512,768]{1,0:T(8,128)(2,1)S(1)}) custom-call(bf16[512,768]{1,0:T(8,128)(2,1)S(1)} %bitcast.13, bf16[768,2304]{1,0:T(8,128)(2,1)S(1)} %copy-done.2, bf16[768,768]{1,0:T(8,128)(2,1)S(1)} %copy-done.4), custom_call_target="tpu_custom_call" | custom-call | flops 3019898880 | bytes 62914560 | tf_op jit(solution)/shard_map/column_stage/pallas_call | solution.py:343
  114.3 0.0 all-gather.3.cloned.1.call-done.up_ref
  114.4 40.5 %all-gather.5.cloned.1.call-done.down_ref = bf16[3072,768]{1,0:T(8,128)(2,1)} async-done(((bf16[192,768]{1,0:T(8,128)(2,1)}), bf16[3072,768]{1,0:T(8,128)(2,1)}) %all-gather.5.cloned.1.call-update) | async-done | bytes 4718608 | tf_op jit(solution)/shard_map/all_gather | solution.py:304
  154.9 12.1 %feed_stage.1 = bf16[512,768]{1,0:T(8,128)(2,1)} custom-call(f32[512,768]{1,0:T(8,128)S(1)} %get-tuple-element.7.x2_ref, bf16[512,768]{1,0:T(8,128)(2,1)S(1)} %get-tuple-element.8.u3_ref, bf16[768,3072]{1,0:T(8,128)(2,1)} %all-gather.3.cloned.1.call-done.up_ref, bf16[3072,768]{1,0:T(8,128)(2,1)} %all-gather.5.cloned.1.call-done.down_ref), custom_call_target="tpu_custom_call" | custom-call | flops 4831838208 | bytes 41943040 | tf_op jit(solution)/shard_map/feed_stage/pallas_call | solution.py:359
Async XLA Ops:
  6.5 107.8 %all-gather.3.cloned.1.call-start = ((), (), s32[]{:S(2)}) async-start(), calls=%async_computation | async-start | bytes 5013504 | tf_op jit(solution)/shard_map/all_gather | solution.py:303
  7.3 147.6 %all-gather.5.cloned.1.call-start = ((), (), s32[]{:S(2)}) async-start(), calls=%async_computation.1 | async-start | bytes 5013504 | tf_op jit(solution)/shard_map/all_gather | solution.py:304
  9.7 0.7 copy-start
  10.3 2.0 %copy-start.1 = (bf16[768,2304]{1,0:T(8,128)(2,1)S(1)}, bf16[768,2304]{1,0:T(8,128)(2,1)}, u32[]{:S(2)}) copy-start(bf16[768,2304]{1,0:T(8,128)(2,1)} %wqkv_ref.2) | copy-start | bytes 10616836
  12.4 1.3 copy-start.3
  13.6 1.1 copy-start.5
  14.8 0.8 copy-start.6
  15.6 0.7 copy-start.7
  16.3 88.5 %copy-start.2 = (bf16[768,2304]{1,0:T(8,128)(2,1)S(1)}, bf16[768,2304]{1,0:T(8,128)(2,1)}, u32[]{:S(2)}) copy-start(bf16[768,2304]{1,0:T(8,128)(2,1)} %wqkv_ref.3) | copy-start | bytes 10616836
  16.3 88.5 %copy-start.4 = (bf16[768,768]{1,0:T(8,128)(2,1)S(1)}, bf16[768,768]{1,0:T(8,128)(2,1)}, u32[]{:S(2)}) copy-start(bf16[768,768]{1,0:T(8,128)(2,1)} %wo_ref.3) | copy-start | bytes 3538948
Sparse Core Ops, SparseCore 0:
  9.6 81.2 all-gather.2
  93.2 61.6 all-gather.4
where the time goes:
time: 174 us
  Pallas kernels  110 us (63%)
  waiting for transfers between devices  41.9 us (24%)
  between operations  13.5 us (8%)
  local copies, waits for them, and re-layouts  8.24 us (5%)
    pallas_call x1, Pallas kernels, fast_device(): pl.pallas_call(functools.partial(row_kernel, n, seqs, length, heads, head...  88.5 us
    all_gather x1, waiting for transfers between devices, fast_device(): full_down = lax.all_gather(feed_down_weight, 'depth', axis=0, tiled=True)  40.5 us
    pallas_call x1, Pallas kernels, fast_device(): pl.pallas_call(functools.partial(feed_kernel, all_seqs), out_shape=jax.Sh...  12.1 us
    pallas_call x1, Pallas kernels, fast_device(): pl.pallas_call(functools.partial(column_kernel, all_seqs, heads, head_siz...  9.57 us
    unnamed x18, local copies, waits for them, and re-layouts  7.43 us
  transfers between devices with their start and end apart: 2, of which 1 were waited for; matrix products, arithmetic and copies ran while one was open for 1% of the time, Pallas kernels for 56%

commit v1 on v0

--- a/solution.py
+++ b/solution.py
@@ -36,12 +36,14 @@
     lax.fori_loop(0, weight_ref.shape[1] // step, body, 0)
 
 
-def row_kernel(
+def layer_kernel(
     n, seqs, length, heads, head_size,
-    tok_ref, chain_col, chain_row, state_ref, emb_ref, bias_ref, wqkv_ref, wo_ref,
+    tok_any, chain_any, state_any, emb_any, bias_any, wqkv_any, wo_any, wqkv2_any, wo2_any, up_any, down_any,
     out_ref,
-    x0_ref, qkv_ref, sbuf, rbuf, tbuf, gbuf, pbuf, mix_ref, xbuf,
-    pair_sems, rs_send, rs_recv, ag_send, ag_recv, fw_send, fw_recv, aa_send, aa_recv, local_sem,
+    tok_ref, chain_row, state_ref, emb_ref, bias_ref, wqkv_ref, wo_ref, wqkv2_ref, wo2_ref, up_ref, down_ref,
+    x0_ref, qkv_ref, sbuf, rbuf, tbuf, gbuf, pbuf, mix_ref, xbuf, block_ref,
+    load_sems, pair_sems, rs_send, rs_recv, ag_send, ag_recv, fw_send, fw_recv, aa_send, aa_recv, local_sem,
+    z_send, z_recv, y_send, y_recv, c_send, c_recv,
 ):
     me = lax.axis_index("depth")
     core = lax.rem(me, 2)
@@ -50,6 +52,30 @@
     sibling = me + 1 - 2 * core
     share = length // n
     width = heads * head_size
+    z_size = n // 4
+    my_y = lax.rem(chip, 2)
+    my_z = chip // 2
+
+    loads = [
+        pltpu.make_async_copy(source, target, load_sems.at[k])
+        for k, (source, target) in enumerate(
+            (
+                (up_any, up_ref.at[me]),
+                (down_any, down_ref.at[me]),
+                (tok_any, tok_ref),
+                (emb_any, emb_ref),
+                (state_any, state_ref),
+                (chain_any, chain_row),
+                (bias_any, bias_ref),
+                (wqkv_any, wqkv_ref),
+                (wo_any, wo_ref),
+                (wqkv2_any, wqkv2_ref),
+                (wo2_any, wo2_ref),
+            )
+        )
+    ]
+    for load in loads:
+        load.start()
 
     barrier = pltpu.get_barrier_semaphore()
 
@@ -61,10 +87,107 @@
 
     lax.fori_loop(1, n, greet, 0)
 
-    letters = lax.broadcasted_iota(jnp.int32, (seqs * length, emb_ref.shape[0]), 1)
-    one_hot = jnp.where(tok_ref[...] == letters, 1.0, 0.0).astype(BF)
-    x0_ref[...] = state_ref[...].astype(F32) + dot(one_hot, emb_ref[...])
+    def place(z, y, c):
+        return (z * 2 + y) * 2 + c
+
+    def hop(index, target, send, recv, at):
+        return [
+            pltpu.make_async_remote_copy(
+                src_ref=ref.at[index], dst_ref=ref.at[index],
+                send_sem=send.at[(w,) + at], recv_sem=recv.at[(w,) + at],
+                device_id={"depth": target}, device_id_type=MESH,
+            )
+            for w, ref in ((0, up_ref), (1, down_ref))
+        ]
+
+    def z_hop(step, sign, origin, target):
+        return hop(place(origin, my_y, core), place(target, my_y, core), z_send, z_recv, (0 if sign > 0 else 1, step))
+
+    def y_hop(origin, y):
+        return hop(place(origin, y, core), place(my_z, 1 - my_y, core), y_send, y_recv, (origin,))
+
+    def c_hop(origin, y, c):
+        return hop(place(origin, y, c), sibling, c_send, c_recv, (origin, y))
+
+    def start(copies):
+        for copy in copies:
+            copy.start()
+
+    def wait_recv(copies):
+        for copy in copies:
+            copy.wait_recv()
+
+    def wait_send(copies):
+        for copy in copies:
+            copy.wait_send()
+
+    def on_line(z):
+        return jnp.logical_and(z >= 0, z < z_size)
+
+    def weights_first():
+        for sign in (1, -1):
+
+            @pl.when(on_line(my_z + sign))
+            def _():
+                start(z_hop(1, sign, my_z, my_z + sign))
+
+        start(y_hop(my_z, my_y))
+        start(c_hop(my_z, my_y, core))
+
+    def weights_step(step):
+        for sign in (1, -1):
+            origin = my_z - sign * step
+
+            @pl.when(on_line(origin))
+            def _():
+                wait_recv(z_hop(step, sign, origin, my_z))
+
+                @pl.when(on_line(my_z + sign))
+                def _():
+                    start(z_hop(step + 1, sign, origin, my_z + sign))
+
+                start(y_hop(origin, my_y))
+                start(c_hop(origin, my_y, core))
+
+    def weights_across(k):
+        origin = lax.rem(my_z + k, z_size)
+        wait_recv(y_hop(origin, 1 - my_y))
+        start(c_hop(origin, 1 - my_y, core))
+
+    def weights_ready():
+        for origin in range(z_size):
+            for y in range(2):
+                wait_recv(c_hop(origin, y, 1 - core))
+
+    def weights_drain():
+        for sign in (1, -1):
+            for step in range(1, z_size):
+                origin = my_z - sign * (step - 1)
+
+                @pl.when(jnp.logical_and(on_line(origin), on_line(my_z + sign)))
+                def _():
+                    wait_send(z_hop(step, sign, origin, my_z + sign))
+
+        for origin in range(z_size):
+            wait_send(y_hop(origin, my_y))
+            for y in range(2):
+                wait_send(c_hop(origin, y, core))
+
+    for load in loads[:5]:
+        load.wait()
+    pl.semaphore_wait(barrier, n - 1)
+    weights_first()
+
+    letters = lax.broadcasted_iota(jnp.int32, (emb_ref.shape[0], length), 0)
+    for s in range(seqs):
+        one_hot = jnp.where(tok_ref[s : s + 1, :] == letters, 1.0, 0.0).astype(BF)
+        picked = lax.dot_general(one_hot, emb_ref[...], (((0,), (0,)), ((), ())), preferred_element_type=F32)
+        x0_ref[s * length : (s + 1) * length, :] = (
+            state_ref[s * length : (s + 1) * length, :].astype(F32) + picked
+        )
     u1 = layer_norm(x0_ref[...]).astype(BF)
+    for load in loads[5:]:
+        load.wait()
     project_into(u1, wqkv_ref, qkv_ref, 256)
     low, high = half_masks(2 * head_size)
 
@@ -83,13 +206,13 @@
         return carry
 
     lax.fori_loop(0, heads // 2, scores, 0)
-    pl.semaphore_wait(barrier, n - 1)
 
     swap = pltpu.make_async_remote_copy(
         src_ref=sbuf.at[1 - core], dst_ref=rbuf, send_sem=pair_sems.at[0], recv_sem=pair_sems.at[1],
         device_id={"depth": sibling}, device_id_type=MESH,
     )
     swap.start()
+    weights_step(1)
     swap.wait()
 
     def rs_copy(k):
@@ -106,6 +229,7 @@
         return carry
 
     lax.fori_loop(1, chips, rs_start, 0)
+    weights_across(0)
     total = sbuf[core, chip].astype(F32) + rbuf[chip].astype(F32)
 
     def rs_add(k, total):
@@ -114,10 +238,12 @@
 
     total = lax.fori_loop(1, chips, rs_add, total)
     factor = 1.0 / (math.sqrt(head_size) * math.sqrt(seqs * n))
-    mine = chain_col[pl.ds(pl.multiple_of(me * share, share), share), :]
+    spot = lax.broadcasted_iota(jnp.int32, (share, length), 1)
+    row = lax.broadcasted_iota(jnp.int32, (share, length), 0) + me * share
+    mine = jnp.sum(jnp.where(spot == row, chain_row[...], 0), axis=-1, keepdims=True)
     same = mine == chain_row[...]
     for h in range(heads):
-        tied = total[h] * factor + jnp.where(same, bias_ref[1, h], bias_ref[0, h])
+        tied = total[h] * factor + jnp.where(same, bias_ref[1:2, h : h + 1], bias_ref[0:1, h : h + 1])
         top = jnp.max(tied, axis=-1, keepdims=True)
         weights = jnp.exp(tied - top)
         pbuf[me, h] = (weights / jnp.sum(weights, axis=-1, keepdims=True)).astype(BF)
@@ -142,6 +268,8 @@
 
     lax.fori_loop(1, chips, ag_start, 0)
     fw_copy(0).start()
+    for step in range(2, 3):
+        weights_step(step)
 
     def ag_forward(k, carry):
         ag_copy(k).wait_recv()
@@ -155,6 +283,8 @@
         return carry
 
     lax.fori_loop(0, chips, fw_wait, 0)
+    for step in range(3, z_size):
+        weights_step(step)
 
     def mixing(p, carry):
         v = jnp.concatenate(pair_cols(2, p), axis=1)
@@ -185,7 +315,7 @@
     def aa_copy(k):
         other = lax.rem(me + k, n)
         return pltpu.make_async_remote_copy(
-            src_ref=xbuf.at[other], dst_ref=out_ref.at[me], send_sem=aa_send.at[k], recv_sem=aa_recv.at[k],
+            src_ref=xbuf.at[other], dst_ref=block_ref.at[me], send_sem=aa_send.at[k], recv_sem=aa_recv.at[k],
             device_id={"depth": other}, device_id_type=MESH,
         )
 
@@ -194,9 +324,11 @@
         return carry
 
     lax.fori_loop(1, n, aa_start, 0)
-    keep = pltpu.make_async_copy(xbuf.at[me], out_ref.at[me], local_sem)
+    keep = pltpu.make_async_copy(xbuf.at[me], block_ref.at[me], local_sem)
     keep.start()
     keep.wait()
+    for k in range(1, z_size):
+        weights_across(k)
 
     def drain(k, carry):
         aa_copy(k).wait()
@@ -212,6 +344,17 @@
 
     lax.fori_loop(1, chips, drain_sends, 0)
     fw_copy(0).wait_send()
+
+    rows = seqs * length
+    all_seqs = seqs * n
+    column_part(all_seqs, heads, head_size, block_ref, wqkv2_ref, wo2_ref, x0_ref, qkv_ref, mix_ref)
+    weights_ready()
+    u3 = layer_norm(x0_ref[...]).astype(BF)
+    mix_ref[...] = u3
+    feed_part(mix_ref, up_ref, down_ref, x0_ref)
+    order = column_order(rows, all_seqs, share, True)
+    out_ref[...] = dot(order, x0_ref[...].astype(BF)).astype(BF)
+    weights_drain()
 
 
 def column_order(rows, all_seqs, cols, inverse):
@@ -222,12 +365,10 @@
     return jnp.where(c == (r % all_seqs) * cols + r // all_seqs, 1.0, 0.0).astype(BF)
 
 
-def column_kernel(
-    all_seqs, heads, head_size, x_ref, wqkv_ref, wo_ref, x2_ref, u3_ref, flat_ref, qkv_ref, mix_ref
-):
-    rows, width = x_ref.shape
+def column_part(all_seqs, heads, head_size, block_ref, wqkv_ref, wo_ref, flat_ref, qkv_ref, mix_ref):
+    rows, width = flat_ref.shape
     cols = rows // all_seqs
-    flat_ref[...] = dot(column_order(rows, all_seqs, cols, False), x_ref[...])
+    flat_ref[...] = dot(column_order(rows, all_seqs, cols, False), block_ref[...].reshape(rows, width))
     u2 = layer_norm(flat_ref[...]).astype(BF)
     project_into(u2, wqkv_ref, qkv_ref, 256)
     pair = 2 * head_size
@@ -255,29 +396,23 @@
         return carry
 
     lax.fori_loop(0, rows // group, attend, 0)
-    x2_ref[...] = flat_ref[...] + dot(mix_ref[...], wo_ref[...])
-    u3_ref[...] = layer_norm(x2_ref[...]).astype(BF)
-
-
-def feed_kernel(all_seqs, x2_ref, u3_ref, up_ref, down_ref, out_ref, acc_ref):
-    rows = x2_ref.shape[0]
-    acc_ref[...] = x2_ref[...]
-    step = 512
+    flat_ref[...] += dot(mix_ref[...], wo_ref[...])
+
+
+def feed_part(u3_ref, up_ref, down_ref, acc_ref):
+    n, up_rows, hidden_size = up_ref.shape
+    down_rows, width = down_ref.shape[1:]
+    span = max(d for d in range(1, n + 1) if n % d == 0 and d * down_rows <= 768)
+    step = span * down_rows
 
     def body(t, carry):
         part = pl.ds(pl.multiple_of(t * step, step), step)
-        pre = dot(u3_ref[...], up_ref[:, part])
+        pre = dot(u3_ref[...], up_ref[:, :, part].reshape(n * up_rows, step))
         hidden = (0.5 * pre * (1.0 + lax.erf(pre * math.sqrt(0.5)))).astype(BF)
-        acc_ref[...] += dot(hidden, down_ref[part, :])
-        return carry
-
-    lax.fori_loop(0, up_ref.shape[1] // step, body, 0)
-    order = column_order(rows, all_seqs, rows // all_seqs, True)
-    out_ref[...] = dot(order, acc_ref[...].astype(BF)).astype(BF)
-
-
-def vmem_specs(count):
-    return [pl.BlockSpec(memory_space=pltpu.VMEM)] * count
+        acc_ref[...] += dot(hidden, down_ref[pl.ds(t * span, span)].reshape(step, width))
+        return carry
+
+    lax.fori_loop(0, hidden_size // step, body, 0)
 
 
 def fast_device(
@@ -300,74 +435,54 @@
     share = length // n
     rows = seqs * length
     all_seqs = seqs * n
-    full_up = lax.all_gather(feed_up_weight, "depth", axis=0, tiled=True)
-    full_down = lax.all_gather(feed_down_weight, "depth", axis=0, tiled=True)
     chunk = (heads, share, length)
-    DMA = pltpu.SemaphoreType.DMA
-    block = pl.pallas_call(
-        functools.partial(row_kernel, n, seqs, length, heads, head_size),
-        out_shape=jax.ShapeDtypeStruct((n, seqs, share, width), BF),
-        in_specs=vmem_specs(5) + [pl.BlockSpec(memory_space=pltpu.SMEM)] + vmem_specs(2),
-        out_specs=pl.BlockSpec(memory_space=pltpu.VMEM),
-        scratch_shapes=[
-            pltpu.VMEM((rows, width), F32),
-            pltpu.VMEM((rows, 3 * width), BF),
-            pltpu.VMEM((2, n // 2) + chunk, BF),
-            pltpu.VMEM((n // 2,) + chunk, BF),
-            pltpu.VMEM((n // 2,) + chunk, BF),
-            pltpu.VMEM((n // 2,) + chunk, BF),
-            pltpu.VMEM((n,) + chunk, BF),
-            pltpu.VMEM((rows, width), BF),
-            pltpu.VMEM((n, seqs, share, width), BF),
-            DMA((2,)),
-            DMA((n // 2,)), DMA((n // 2,)), DMA((n // 2,)), DMA((n // 2,)),
-            DMA((n // 2,)), DMA((n // 2,)), DMA((n,)), DMA((n,)), DMA,
-        ],
-        compiler_params=pltpu.CompilerParams(
-            collective_id=0, has_side_effects=True, vmem_limit_bytes=40 * 2**20
-        ),
-        cost_estimate=pl.CostEstimate(
-            flops=2 * rows * width * width * 5, bytes_accessed=200 * 2**20, transcendentals=0
-        ),
-        name="row_stage",
-    )(
-        alignment_token_grid.reshape(rows, 1),
-        residue_chain_index.reshape(length, 1),
+    arrays = (
+        alignment_token_grid,
         residue_chain_index.reshape(1, length),
         alignment_state.reshape(rows, width),
         embedding,
         chain_head_bias,
         row_query_key_value,
         row_output_weight,
-    )
-    x2, u3 = pl.pallas_call(
-        functools.partial(column_kernel, all_seqs, heads, head_size),
-        out_shape=(jax.ShapeDtypeStruct((rows, width), F32), jax.ShapeDtypeStruct((rows, width), BF)),
-        in_specs=vmem_specs(3),
-        out_specs=(pl.BlockSpec(memory_space=pltpu.VMEM),) * 2,
-        scratch_shapes=[
+        column_query_key_value,
+        column_output_weight,
+    )
+    DMA = pltpu.SemaphoreType.DMA
+    half = n // 2
+    deep = n // 4
+    result = pl.pallas_call(
+        functools.partial(layer_kernel, n, seqs, length, heads, head_size),
+        out_shape=jax.ShapeDtypeStruct((rows, width), BF),
+        in_specs=[pl.BlockSpec(memory_space=pl.ANY)] * 11,
+        out_specs=pl.BlockSpec(memory_space=pltpu.VMEM),
+        scratch_shapes=[pltpu.VMEM(x.shape, x.dtype) for x in arrays]
+        + [
+            pltpu.VMEM((n,) + feed_up_weight.shape, BF),
+            pltpu.VMEM((n,) + feed_down_weight.shape, BF),
             pltpu.VMEM((rows, width), F32),
             pltpu.VMEM((rows, 3 * width), BF),
+            pltpu.VMEM((2, half) + chunk, BF),
+            pltpu.VMEM((half,) + chunk, BF),
+            pltpu.VMEM((half,) + chunk, BF),
+            pltpu.VMEM((half,) + chunk, BF),
+            pltpu.VMEM((n,) + chunk, BF),
             pltpu.VMEM((rows, width), BF),
+            pltpu.VMEM((n, seqs, share, width), BF),
+            pltpu.VMEM((n, seqs, share, width), BF),
+            DMA((11,)), DMA((2,)),
+            DMA((half,)), DMA((half,)), DMA((half,)), DMA((half,)),
+            DMA((half,)), DMA((half,)), DMA((n,)), DMA((n,)), DMA,
+            DMA((2, 2, deep)), DMA((2, 2, deep)), DMA((2, deep)), DMA((2, deep)),
+            DMA((2, deep, 2)), DMA((2, deep, 2)),
         ],
-        compiler_params=pltpu.CompilerParams(vmem_limit_bytes=40 * 2**20),
+        compiler_params=pltpu.CompilerParams(
+            collective_id=0, has_side_effects=True, vmem_limit_bytes=58 * 2**20
+        ),
         cost_estimate=pl.CostEstimate(
-            flops=2 * rows * width * width * 5, bytes_accessed=60 * 2**20, transcendentals=0
+            flops=2 * rows * width * width * 18, bytes_accessed=40 * 2**20, transcendentals=0
         ),
-        name="column_stage",
-    )(block.reshape(rows, width), column_query_key_value, column_output_weight)
-    result = pl.pallas_call(
-        functools.partial(feed_kernel, all_seqs),
-        out_shape=jax.ShapeDtypeStruct((rows, width), BF),
-        in_specs=vmem_specs(4),
-        out_specs=pl.BlockSpec(memory_space=pltpu.VMEM),
-        scratch_shapes=[pltpu.VMEM((rows, width), F32)],
-        compiler_params=pltpu.CompilerParams(vmem_limit_bytes=48 * 2**20),
-        cost_estimate=pl.CostEstimate(
-            flops=2 * rows * width * width * 8, bytes_accessed=40 * 2**20, transcendentals=0
-        ),
-        name="feed_stage",
-    )(x2, u3, full_up, full_down)
+        name="layer",
+    )(*arrays, feed_up_weight, feed_down_weight)
     return result.reshape(all_seqs, share, width)
 
 
@@ -476,6 +591,9 @@
         n % 2 == 0
         and length % n == 0
         and (length // n) % 16 == 0
+        and n % 4 == 0
+        and arrays[9].shape[0] % 16 == 0
+        and arrays[10].shape[0] % 64 == 0
         and 128 % (seqs * n) == 0
         and (seqs * length) % 128 == 0
         and 2 * (width // heads) == 128

time: 174 us -> 126 us (0.72)
  waiting for transfers between devices: 41.9 us -> 0 us
  between operations: 13.5 us -> 0.01 us
  Pallas kernels: 110 us -> 123 us
  local copies, waits for them, and re-layouts: 8.24 us -> 2.06 us
    all_gather x2 -> x0, waiting for transfers between devices: 40.5 us -> none  [the longest x1 40.5 us: fast_device(): full_down = lax.all_gather(feed_down_weight, 'depth', axis=0, tiled=True)]
    pallas_call x3 -> x1, Pallas kernels: 110 us -> 123 us  [fast_device(): pl.pallas_call(functools.partial(layer_kernel, n, seqs, length, heads, he...]
    unnamed x18 -> x1, local copies, waits for them, and re-layouts: 7.43 us -> 2.06 us
  transfers between devices with their start and end apart: 2 -> 0, of which waited for: 1 -> 0; matrix products, arithmetic and copies ran while one was open for 1% -> 0% of each run, Pallas kernels for 56% -> 0%
where the time goes in v1:
time: 126 us
  Pallas kernels  123 us (98%)
  local copies, waits for them, and re-layouts  2.06 us (2%)
    pallas_call x1, Pallas kernels, fast_device(): pl.pallas_call(functools.partial(layer_kernel, n, seqs, length, heads, he...  123 us

profile of v1, /device:TPU:0, one launch (start us, length us, event | category | flops | bytes accessed | tf_op | source)
XLA Modules:
  0.0 125.5 jit_solution(17107828627989956746)
XLA Ops:
  0.0 123.4 %layer.1 = bf16[512,768]{1,0:T(8,128)(2,1)} custom-call(s32[2,256]{1,0:T(2,128)} %tok_any.1, s32[1,256]{1,0:T(1,128)} %bitcast.5, bf16[512,768]{1,0:T(8,128)(2,1)} %bitcast.4, bf16[33,768]{1,0:T(8,128)(2,1)} %emb_any.1, f32[2,12]{1,0:T(2,128)} %bias_any.1, bf16[768,2304]{1,0:T(8,128)(2,1)} %wqkv_any.1, bf16[768,768]{1,0:T(8,128)(2,1)} %wo_any.1, ...), custom_call_target="tpu_custom_call" | custom-call | flops 10871635968 | bytes 41943040 | tf_op jit(solution)/shard_map/layer/pallas_call | solution.py:453
  123.4 2.1 %copy.13 = bf16[32,16,768]{2,1,0:T(8,128)(2,1)} copy(bf16[32,16,768]{2,1,0:T(8,128)(2,1)} %bitcast.3) | data formatting | bytes 1572864

commit v2 on v1

--- a/solution.py
+++ b/solution.py
@@ -43,7 +43,7 @@
     tok_ref, chain_row, state_ref, emb_ref, bias_ref, wqkv_ref, wo_ref, wqkv2_ref, wo2_ref, up_ref, down_ref,
     x0_ref, qkv_ref, sbuf, rbuf, tbuf, gbuf, pbuf, mix_ref, xbuf, block_ref,
     load_sems, pair_sems, rs_send, rs_recv, ag_send, ag_recv, fw_send, fw_recv, aa_send, aa_recv, local_sem,
-    z_send, z_recv, y_send, y_recv, c_send, c_recv,
+    z_send, z_recv, y_send, y_recv, c_send, c_recv, x_send, x_recv,
 ):
     me = lax.axis_index("depth")
     core = lax.rem(me, 2)
@@ -55,6 +55,7 @@
     z_size = n // 4
     my_y = lax.rem(chip, 2)
     my_z = chip // 2
+    group = lax.axis_index("groups")
 
     loads = [
         pltpu.make_async_copy(source, target, load_sems.at[k])
@@ -86,6 +87,7 @@
         return carry
 
     lax.fori_loop(1, n, greet, 0)
+    pl.semaphore_signal(barrier, inc=1, device_id={"groups": 1 - group}, device_id_type=MESH)
 
     def place(z, y, c):
         return (z * 2 + y) * 2 + c
@@ -95,7 +97,8 @@
             pltpu.make_async_remote_copy(
                 src_ref=ref.at[index], dst_ref=ref.at[index],
                 send_sem=send.at[(w,) + at], recv_sem=recv.at[(w,) + at],
-                device_id={"depth": target}, device_id_type=MESH,
+                device_id=target if isinstance(target, dict) else {"depth": target},
+                device_id_type=MESH,
             )
             for w, ref in ((0, up_ref), (1, down_ref))
         ]
@@ -109,17 +112,20 @@
     def c_hop(origin, y, c):
         return hop(place(origin, y, c), sibling, c_send, c_recv, (origin, y))
 
-    def start(copies):
-        for copy in copies:
-            copy.start()
-
-    def wait_recv(copies):
-        for copy in copies:
-            copy.wait_recv()
-
-    def wait_send(copies):
-        for copy in copies:
-            copy.wait_send()
+    def x_hop(origin, y):
+        return hop(place(origin, y, core), {"groups": 1 - group}, x_send, x_recv, (origin, y))
+
+    def start(copies, mine=True):
+        for w, copy in enumerate(copies):
+            pl.when(group == (w if mine else 1 - w))(copy.start)
+
+    def wait_recv(copies, mine=True):
+        for w, copy in enumerate(copies):
+            pl.when(group == (w if mine else 1 - w))(copy.wait_recv)
+
+    def wait_send(copies, mine=True):
+        for w, copy in enumerate(copies):
+            pl.when(group == (w if mine else 1 - w))(copy.wait_send)
 
     def on_line(z):
         return jnp.logical_and(z >= 0, z < z_size)
@@ -133,6 +139,7 @@
 
         start(y_hop(my_z, my_y))
         start(c_hop(my_z, my_y, core))
+        start(c_hop(my_z, my_y, core), False)
 
     def weights_step(step):
         for sign in (1, -1):
@@ -147,17 +154,25 @@
                     start(z_hop(step + 1, sign, origin, my_z + sign))
 
                 start(y_hop(origin, my_y))
+                start(x_hop(origin, my_y))
                 start(c_hop(origin, my_y, core))
 
     def weights_across(k):
         origin = lax.rem(my_z + k, z_size)
         wait_recv(y_hop(origin, 1 - my_y))
+        start(x_hop(origin, 1 - my_y))
         start(c_hop(origin, 1 - my_y, core))
+
+    def weights_cross(k, y):
+        origin = lax.rem(my_z + k, z_size)
+        wait_recv(x_hop(origin, y), False)
+        start(c_hop(origin, y, core), False)
 
     def weights_ready():
         for origin in range(z_size):
             for y in range(2):
-                wait_recv(c_hop(origin, y, 1 - core))
+                for mine in (True, False):
+                    wait_recv(c_hop(origin, y, 1 - core), mine)
 
     def weights_drain():
         for sign in (1, -1):
@@ -170,12 +185,16 @@
 
         for origin in range(z_size):
             wait_send(y_hop(origin, my_y))
+            wait_send(x_hop(origin, 1 - my_y))
             for y in range(2):
-                wait_send(c_hop(origin, y, core))
+                for mine in (True, False):
+                    wait_send(c_hop(origin, y, core), mine)
+        for k in range(1, z_size):
+            wait_send(x_hop(lax.rem(my_z + k, z_size), my_y))
 
     for load in loads[:5]:
         load.wait()
-    pl.semaphore_wait(barrier, n - 1)
+    pl.semaphore_wait(barrier, n)
     weights_first()
 
     letters = lax.broadcasted_iota(jnp.int32, (emb_ref.shape[0], length), 0)
@@ -215,28 +234,47 @@
     weights_step(1)
     swap.wait()
 
+    def rs_y_copy(z):
+        return pltpu.make_async_remote_copy(
+            src_ref=tbuf.at[z_size + z], dst_ref=gbuf.at[z_size + z],
+            send_sem=rs_send.at[z_size + z], recv_sem=rs_recv.at[z_size + z],
+            device_id={"depth": place(my_z, 1 - my_y, core)}, device_id_type=MESH,
+        )
+
     def rs_copy(k):
-        other = lax.rem(chip + k, chips)
         return pltpu.make_async_remote_copy(
-            src_ref=tbuf.at[other], dst_ref=gbuf.at[k], send_sem=rs_send.at[k], recv_sem=rs_recv.at[k],
-            device_id={"depth": other * 2 + core}, device_id_type=MESH,
-        )
+            src_ref=tbuf.at[k], dst_ref=gbuf.at[k], send_sem=rs_send.at[k], recv_sem=rs_recv.at[k],
+            device_id={"depth": place(lax.rem(my_z + k, z_size), my_y, core)}, device_id_type=MESH,
+        )
+
+    def rs_y_start(k, carry):
+        z = lax.rem(my_z + k, z_size)
+        at = z * 2 + 1 - my_y
+        tbuf[z_size + z] = (sbuf[core, at].astype(F32) + rbuf[at].astype(F32)).astype(BF)
+        rs_y_copy(z).start()
+        return carry
+
+    lax.fori_loop(1, z_size + 1, rs_y_start, 0)
+
+    def chips_sum(z):
+        at = z * 2 + my_y
+        rs_y_copy(z).wait_recv()
+        return sbuf[core, at].astype(F32) + rbuf[at].astype(F32) + gbuf[z_size + z].astype(F32)
 
     def rs_start(k, carry):
-        other = lax.rem(chip + k, chips)
-        tbuf[other] = (sbuf[core, other].astype(F32) + rbuf[other].astype(F32)).astype(BF)
+        tbuf[k] = chips_sum(lax.rem(my_z + k, z_size)).astype(BF)
         rs_copy(k).start()
         return carry
 
-    lax.fori_loop(1, chips, rs_start, 0)
+    lax.fori_loop(1, z_size, rs_start, 0)
     weights_across(0)
-    total = sbuf[core, chip].astype(F32) + rbuf[chip].astype(F32)
+    total = chips_sum(my_z)
 
     def rs_add(k, total):
         rs_copy(k).wait_recv()
         return total + gbuf[k].astype(F32)
 
-    total = lax.fori_loop(1, chips, rs_add, total)
+    total = lax.fori_loop(1, z_size, rs_add, total)
     factor = 1.0 / (math.sqrt(head_size) * math.sqrt(seqs * n))
     spot = lax.broadcasted_iota(jnp.int32, (share, length), 1)
     row = lax.broadcasted_iota(jnp.int32, (share, length), 0) + me * share
@@ -249,16 +287,27 @@
         pbuf[me, h] = (weights / jnp.sum(weights, axis=-1, keepdims=True)).astype(BF)
 
     def ag_copy(k):
-        other = lax.rem(chip + k, chips)
         return pltpu.make_async_remote_copy(
             src_ref=pbuf.at[me], dst_ref=pbuf.at[me], send_sem=ag_send.at[k], recv_sem=ag_recv.at[k],
-            device_id={"depth": other * 2 + core}, device_id_type=MESH,
-        )
-
-    def fw_copy(k):
-        origin = lax.rem(chip - k + chips, chips) * 2 + core
+            device_id={"depth": place(lax.rem(my_z + k, z_size), my_y, core)}, device_id_type=MESH,
+        )
+
+    def back(k):
+        return lax.rem(my_z - k + z_size, z_size)
+
+    def ag_y_copy(k):
+        origin = place(back(k), my_y, core)
         return pltpu.make_async_remote_copy(
-            src_ref=pbuf.at[origin], dst_ref=pbuf.at[origin], send_sem=fw_send.at[k], recv_sem=fw_recv.at[k],
+            src_ref=pbuf.at[origin], dst_ref=pbuf.at[origin],
+            send_sem=ag_send.at[z_size + k], recv_sem=ag_recv.at[z_size + k],
+            device_id={"depth": place(my_z, 1 - my_y, core)}, device_id_type=MESH,
+        )
+
+    def fw_copy(k, far):
+        origin = place(back(k), 1 - my_y if far else my_y, core)
+        at = z_size + k if far else k
+        return pltpu.make_async_remote_copy(
+            src_ref=pbuf.at[origin], dst_ref=pbuf.at[origin], send_sem=fw_send.at[at], recv_sem=fw_recv.at[at],
             device_id={"depth": sibling}, device_id_type=MESH,
         )
 
@@ -266,23 +315,33 @@
         ag_copy(k).start()
         return carry
 
-    lax.fori_loop(1, chips, ag_start, 0)
-    fw_copy(0).start()
+    lax.fori_loop(1, z_size, ag_start, 0)
+    ag_y_copy(0).start()
+    fw_copy(0, False).start()
+
+    def ag_forward(k, carry):
+        ag_copy(k).wait_recv()
+        ag_y_copy(k).start()
+        fw_copy(k, False).start()
+        return carry
+
+    lax.fori_loop(1, z_size, ag_forward, 0)
     for step in range(2, 3):
         weights_step(step)
 
-    def ag_forward(k, carry):
-        ag_copy(k).wait_recv()
-        fw_copy(k).start()
-        return carry
-
-    lax.fori_loop(1, chips, ag_forward, 0)
+    def ag_y_forward(k, carry):
+        ag_y_copy(k).wait_recv()
+        fw_copy(k, True).start()
+        return carry
+
+    lax.fori_loop(0, z_size, ag_y_forward, 0)
 
     def fw_wait(k, carry):
-        fw_copy(k).wait_recv()
-        return carry
-
-    lax.fori_loop(0, chips, fw_wait, 0)
+        fw_copy(k, False).wait_recv()
+        fw_copy(k, True).wait_recv()
+        return carry
+
+    lax.fori_loop(0, z_size, fw_wait, 0)
     for step in range(3, z_size):
         weights_step(step)
 
@@ -329,6 +388,8 @@
     keep.wait()
     for k in range(1, z_size):
         weights_across(k)
+    for k in range(1, z_size):
+        weights_cross(k, my_y)
 
     def drain(k, carry):
         aa_copy(k).wait()
@@ -339,15 +400,26 @@
     def drain_sends(k, carry):
         rs_copy(k).wait_send()
         ag_copy(k).wait_send()
-        fw_copy(k).wait_send()
-        return carry
-
-    lax.fori_loop(1, chips, drain_sends, 0)
-    fw_copy(0).wait_send()
+        return carry
+
+    lax.fori_loop(1, z_size, drain_sends, 0)
+
+    def drain_more(k, carry):
+        rs_y_copy(k).wait_send()
+        ag_y_copy(k).wait_send()
+        fw_copy(k, False).wait_send()
+        fw_copy(k, True).wait_send()
+        return carry
+
+    lax.fori_loop(0, z_size, drain_more, 0)
+
+    def between():
+        for k in range(z_size):
+            weights_cross(k, 1 - my_y)
 
     rows = seqs * length
     all_seqs = seqs * n
-    column_part(all_seqs, heads, head_size, block_ref, wqkv2_ref, wo2_ref, x0_ref, qkv_ref, mix_ref)
+    column_part(all_seqs, heads, head_size, block_ref, wqkv2_ref, wo2_ref, x0_ref, qkv_ref, mix_ref, between)
     weights_ready()
     u3 = layer_norm(x0_ref[...]).astype(BF)
     mix_ref[...] = u3
@@ -365,12 +437,13 @@
     return jnp.where(c == (r % all_seqs) * cols + r // all_seqs, 1.0, 0.0).astype(BF)
 
 
-def column_part(all_seqs, heads, head_size, block_ref, wqkv_ref, wo_ref, flat_ref, qkv_ref, mix_ref):
+def column_part(all_seqs, heads, head_size, block_ref, wqkv_ref, wo_ref, flat_ref, qkv_ref, mix_ref, between):
     rows, width = flat_ref.shape
     cols = rows // all_seqs
     flat_ref[...] = dot(column_order(rows, all_seqs, cols, False), block_ref[...].reshape(rows, width))
     u2 = layer_norm(flat_ref[...]).astype(BF)
     project_into(u2, wqkv_ref, qkv_ref, 256)
+    between()
     pair = 2 * head_size
     low, high = half_masks(pair)
     group = 128
@@ -473,7 +546,7 @@
             DMA((half,)), DMA((half,)), DMA((half,)), DMA((half,)),
             DMA((half,)), DMA((half,)), DMA((n,)), DMA((n,)), DMA,
             DMA((2, 2, deep)), DMA((2, 2, deep)), DMA((2, deep)), DMA((2, deep)),
-            DMA((2, deep, 2)), DMA((2, deep, 2)),
+            DMA((2, deep, 2)), DMA((2, deep, 2)), DMA((2, deep, 2)), DMA((2, deep, 2)),
         ],
         compiler_params=pltpu.CompilerParams(
             collective_id=0, has_side_effects=True, vmem_limit_bytes=58 * 2**20
@@ -592,6 +665,8 @@
         and length % n == 0
         and (length // n) % 16 == 0
         and n % 4 == 0
+        and n >= 16
+        and lax.axis_size("groups") == 2
         and arrays[9].shape[0] % 16 == 0
         and arrays[10].shape[0] % 64 == 0
         and 128 % (seqs * n) == 0

time: 126 us -> 104 us (0.83)
  the two profiles are of different devices: /device:TPU:0 before, /device:TPU:24 now
where the time goes in v2:
time: 104 us; the launch traced here: 103 us
  Pallas kernels  101 us (97%)
  local copies, waits for them, and re-layouts  2.06 us (2%)
    pallas_call x1, Pallas kernels, fast_device(): pl.pallas_call(functools.partial(layer_kernel, n, seqs, length, heads, he...  101 us

profile of v2, /device:TPU:24, one launch (start us, length us, event | category | flops | bytes accessed | tf_op | source)
XLA Modules:
  0.0 103.4 jit_solution(2052681173975832670)
XLA Ops:
  0.0 101.3 %layer.1 = bf16[512,768]{1,0:T(8,128)(2,1)} custom-call(s32[2,256]{1,0:T(2,128)} %tok_any.1, s32[1,256]{1,0:T(1,128)} %bitcast.5, bf16[512,768]{1,0:T(8,128)(2,1)} %bitcast.4, bf16[33,768]{1,0:T(8,128)(2,1)} %emb_any.1, f32[2,12]{1,0:T(2,128)} %bias_any.1, bf16[768,2304]{1,0:T(8,128)(2,1)} %wqkv_any.1, bf16[768,768]{1,0:T(8,128)(2,1)} %wo_any.1, ...), custom_call_target="tpu_custom_call" | custom-call | flops 10871635968 | bytes 41943040 | tf_op jit(solution)/shard_map/layer/pallas_call | solution.py:526
  101.3 2.1 %copy.13 = bf16[32,16,768]{2,1,0:T(8,128)(2,1)} copy(bf16[32,16,768]{2,1,0:T(8,128)(2,1)} %bitcast.3) | data formatting | bytes 1572864

commit v3 on v2

--- a/solution.py
+++ b/solution.py
@@ -388,8 +388,6 @@
     keep.wait()
     for k in range(1, z_size):
         weights_across(k)
-    for k in range(1, z_size):
-        weights_cross(k, my_y)
 
     def drain(k, carry):
         aa_copy(k).wait()
@@ -414,6 +412,8 @@
     lax.fori_loop(0, z_size, drain_more, 0)
 
     def between():
+        for k in range(1, z_size):
+            weights_cross(k, my_y)
         for k in range(z_size):
             weights_cross(k, 1 - my_y)
 

time: 104 us -> 104 us (level)
  no operation moved by 1% of the time
where the time goes in v3:
time: 104 us; the launch traced here: 103 us
  Pallas kernels  101 us (97%)
  local copies, waits for them, and re-layouts  2.06 us (2%)
    pallas_call x1, Pallas kernels, fast_device(): pl.pallas_call(functools.partial(layer_kernel, n, seqs, length, heads, he...  101 us

profile of v3, /device:TPU:24, one launch (start us, length us, event | category | flops | bytes accessed | tf_op | source)
XLA Modules:
  0.0 103.4 jit_solution(15049092539800880375)
XLA Ops:
  0.0 101.3 %layer.1 = bf16[512,768]{1,0:T(8,128)(2,1)} custom-call(s32[2,256]{1,0:T(2,128)} %tok_any.1, s32[1,256]{1,0:T(1,128)} %bitcast.5, bf16[512,768]{1,0:T(8,128)(2,1)} %bitcast.4, bf16[33,768]{1,0:T(8,128)(2,1)} %emb_any.1, f32[2,12]{1,0:T(2,128)} %bias_any.1, bf16[768,2304]{1,0:T(8,128)(2,1)} %wqkv_any.1, bf16[768,768]{1,0:T(8,128)(2,1)} %wo_any.1, ...), custom_call_target="tpu_custom_call" | custom-call | flops 10871635968 | bytes 41943040 | tf_op jit(solution)/shard_map/layer/pallas_call | solution.py:526
  101.3 2.1 %copy.13 = bf16[32,16,768]{2,1,0:T(8,128)(2,1)} copy(bf16[32,16,768]{2,1,0:T(8,128)(2,1)} %bitcast.3) | data formatting | bytes 1572864
